TPU v7x, 32 devices: a whole 2x2x4 slice. The times are simulated.
32 devices in a mesh: row: 8 (over z, y), col: 4 (over x, core).
Axes of the slice: x: 2, y: 2, z: 4, core: 2. Of those that a mesh axis runs over, the one named last changes fastest.
Arguments:
- panel: float32 [131072, 256], P(('row', 'col')), may hold values from -36 to 36, as said below
Outputs:
- basis: float32 [131072, 256], P(('row', 'col'))
- factor: float32 [256, 256], replicated
Inputs may be any that keep to these rules, and one draw needn't show every extreme that they name: `panel`: columns have mixed scales; entries are of order one to some tens.
All inputs are finite; a program needn't handle non-finite values.
Results may differ from a plain program's by a relative error of at most 0.0003.
Values sent between devices are 32-bit elements; how exact they have to be, the bound alone decides.
A program may use at most 128 MiB of HBM per device.

v0:
```python
import jax
import jax.numpy as jnp
from jax import lax
from jax.sharding import PartitionSpec as P


def from_partner(value, axis, stride):
    mask = 2**stride
    pairs = [(source, source ^ mask) for source in range(lax.axis_size(axis))]
    return lax.ppermute(value, axis, pairs)


def gram_of(matrix):
    return lax.dot_general(
        matrix,
        matrix,
        (((0,), (0,)), ((), ())),
        precision=lax.Precision.HIGHEST,
        preferred_element_type=jnp.float32,
    )


def whiten(matrix, lower):
    return jax.scipy.linalg.solve_triangular(lower, matrix.T, lower=True).T


def product(left, right):
    return jnp.dot(left, right, precision=lax.Precision.HIGHEST)


def merge_pair(upper, partner, accum):
    lower_one = jnp.linalg.cholesky(gram_of(upper) + gram_of(partner))
    own_one = whiten(upper, lower_one)
    other_one = whiten(partner, lower_one)
    lower_two = jnp.linalg.cholesky(gram_of(own_one) + gram_of(other_one))
    own_two = whiten(own_one, lower_two)
    return (product(lower_two.T, lower_one.T), product(accum, own_two))


def on_device(panel):
    scale = jnp.sqrt(jnp.float32(panel.shape[0] * lax.axis_size("row") * lax.axis_size("col")))
    lower_one = jnp.linalg.cholesky(gram_of(panel))
    first = whiten(panel, lower_one)
    lower_two = jnp.linalg.cholesky(gram_of(first))
    local_q = whiten(first, lower_two)
    local_r = product(lower_two.T, lower_one.T)
    upper = local_r
    accum = jnp.eye(panel.shape[1], dtype=jnp.float32)
    for bit in range(lax.axis_size("row").bit_length() - 1):
        partner = from_partner(upper, "row", bit)
        upper, accum = merge_pair(upper, partner, accum)
    for bit in range(lax.axis_size("col").bit_length() - 1):
        partner = from_partner(upper, "col", bit)
        upper, accum = merge_pair(upper, partner, accum)
    result = product(local_q, accum)
    return (result * scale, upper / scale)


def solution(mesh):
    return jax.shard_map(
        on_device,
        mesh=mesh,
        in_specs=(P(("row", "col"), None),),
        out_specs=(P(("row", "col"), None), P()),
        check_vma=False,
    )
```

profile of v0, /device:TPU:0, one launch (start us, length us, event | category | flops | bytes accessed | tf_op | source)
XLA Modules:
  0.0 830.7 jit_solution(17712042251412341112)
XLA Ops:
  0.6 10.1 %fusion.267 = f32[256,256]{1,0:T(8,128)S(1)} fusion(f32[4096,256]{1,0:T(8,128)} %param.6), kind=kOutput, calls=%fused_computation.463 | convolution fusion | flops 3221225472 | bytes 4456448 | tf_op jit(solution)/shard_map/dot_general | solution.py:14
  10.9 11.7 %cholesky.550 = f32[128,128]{1,0:T(8,128)S(1)} custom-call(f32[128,128]{1,0:T(8,128)S(1)} %cholesky.954), custom_call_target="Cholesky" | custom-call | tf_op jit(solution)/shard_map/jit(cholesky)/cholesky | solution.py:42
  22.7 9.8 %custom-call.40 = f32[1,128,128]{1,2,0:T(8,128)S(1)} custom-call(f32[1,128,128]{2,1,0:T(8,128)S(1)} %get-tuple-element.295), custom_call_target="InvertDiagBlocksLowerTriangular" | custom-call | tf_op jit(solution)/shard_map/jit(cholesky)/cholesky | solution.py:42
  33.0 11.7 %cholesky.567 = f32[128,128]{1,0:T(8,128)S(1)} custom-call(f32[128,128]{1,0:T(8,128)S(1)} %convolution_subtract_fusion.18), custom_call_target="Cholesky" | custom-call | tf_op jit(solution)/shard_map/jit(cholesky)/cholesky | solution.py:42
  46.8 4.1 while.34
  50.9 20.1 %custom-call.41 = f32[2,128,128]{1,2,0:T(8,128)S(1)} custom-call(f32[2,128,128]{2,1,0:T(8,128)S(1)} %get-tuple-element.111), custom_call_target="InvertDiagBlocksLowerTriangular" | custom-call | tf_op jit(solution)/shard_map/jit(_solve_triangular)/triangular_solve | solution.py:24
  85.3 11.9 %cholesky.584 = f32[128,128]{1,0:T(8,128)S(1)} custom-call(f32[128,128]{1,0:T(8,128)S(1)} %cholesky.957), custom_call_target="Cholesky" | custom-call | tf_op jit(solution)/shard_map/jit(cholesky)/cholesky | solution.py:44
  97.9 9.8 %custom-call.42 = f32[1,128,128]{1,2,0:T(8,128)S(1)} custom-call(f32[1,128,128]{2,1,0:T(8,128)S(1)} %get-tuple-element.291), custom_call_target="InvertDiagBlocksLowerTriangular" | custom-call | tf_op jit(solution)/shard_map/jit(cholesky)/cholesky | solution.py:44
  108.2 11.7 %cholesky.601 = f32[128,128]{1,0:T(8,128)S(1)} custom-call(f32[128,128]{1,0:T(8,128)S(1)} %convolution_subtract_fusion.17), custom_call_target="Cholesky" | custom-call | tf_op jit(solution)/shard_map/jit(cholesky)/cholesky | solution.py:44
  125.5 4.1 while.35
  129.5 19.9 %custom-call.43 = f32[2,128,128]{1,2,0:T(8,128)S(1)} custom-call(f32[2,128,128]{2,1,0:T(8,128)S(1)} %get-tuple-element.112), custom_call_target="InvertDiagBlocksLowerTriangular" | custom-call | tf_op jit(solution)/shard_map/jit(_solve_triangular)/triangular_solve | solution.py:24
  158.1 11.7 %cholesky.618 = f32[128,128]{1,0:T(8,128)S(1)} custom-call(f32[128,128]{1,0:T(8,128)S(1)} %cholesky.960), custom_call_target="Cholesky" | custom-call | tf_op jit(solution)/shard_map/jit(cholesky)/cholesky | solution.py:32
  170.5 10.2 %custom-call.44 = f32[1,128,128]{1,2,0:T(8,128)S(1)} custom-call(f32[1,128,128]{2,1,0:T(8,128)S(1)} %get-tuple-element.287), custom_call_target="InvertDiagBlocksLowerTriangular" | custom-call | tf_op jit(solution)/shard_map/jit(cholesky)/cholesky | solution.py:32
  181.2 11.7 %cholesky.635 = f32[128,128]{1,0:T(8,128)S(1)} custom-call(f32[128,128]{1,0:T(8,128)S(1)} %slice_subtract_fusion.14), custom_call_target="Cholesky" | custom-call | tf_op jit(solution)/shard_map/jit(cholesky)/cholesky | solution.py:32
  195.0 4.1 while.36
  199.0 19.9 %custom-call.45 = f32[2,128,128]{1,2,0:T(8,128)S(1)} custom-call(f32[2,128,128]{2,1,0:T(8,128)S(1)} %get-tuple-element.113), custom_call_target="InvertDiagBlocksLowerTriangular" | custom-call | tf_op jit(solution)/shard_map/jit(_solve_triangular)/triangular_solve | solution.py:24
  222.0 11.7 %cholesky.652 = f32[128,128]{1,0:T(8,128)S(1)} custom-call(f32[128,128]{1,0:T(8,128)S(1)} %cholesky.963), custom_call_target="Cholesky" | custom-call | tf_op jit(solution)/shard_map/jit(cholesky)/cholesky | solution.py:35
  234.4 9.8 %custom-call.47 = f32[1,128,128]{1,2,0:T(8,128)S(1)} custom-call(f32[1,128,128]{2,1,0:T(8,128)S(1)} %get-tuple-element.283), custom_call_target="InvertDiagBlocksLowerTriangular" | custom-call | tf_op jit(solution)/shard_map/jit(cholesky)/cholesky | solution.py:35
  244.7 12.1 %cholesky.669 = f32[128,128]{1,0:T(8,128)S(1)} custom-call(f32[128,128]{1,0:T(8,128)S(1)} %convolution_subtract_fusion.16), custom_call_target="Cholesky" | custom-call | tf_op jit(solution)/shard_map/jit(cholesky)/cholesky | solution.py:35
  259.4 4.0 while.37
  263.4 19.7 %custom-call.48 = f32[2,128,128]{1,2,0:T(8,128)S(1)} custom-call(f32[2,128,128]{2,1,0:T(8,128)S(1)} %get-tuple-element.115), custom_call_target="InvertDiagBlocksLowerTriangular" | custom-call | tf_op jit(solution)/shard_map/jit(_solve_triangular)/triangular_solve | solution.py:24
  286.5 5.3 collective-permute-done.1
  292.6 11.7 %cholesky.686 = f32[128,128]{1,0:T(8,128)S(1)} custom-call(f32[128,128]{1,0:T(8,128)S(1)} %cholesky.966), custom_call_target="Cholesky" | custom-call | tf_op jit(solution)/shard_map/jit(cholesky)/cholesky | solution.py:32
  305.0 9.8 %custom-call.49 = f32[1,128,128]{1,2,0:T(8,128)S(1)} custom-call(f32[1,128,128]{2,1,0:T(8,128)S(1)} %get-tuple-element.279), custom_call_target="InvertDiagBlocksLowerTriangular" | custom-call | tf_op jit(solution)/shard_map/jit(cholesky)/cholesky | solution.py:32
  315.3 11.9 %cholesky.703 = f32[128,128]{1,0:T(8,128)S(1)} custom-call(f32[128,128]{1,0:T(8,128)S(1)} %slice_subtract_fusion.13), custom_call_target="Cholesky" | custom-call | tf_op jit(solution)/shard_map/jit(cholesky)/cholesky | solution.py:32
  329.3 4.1 while.38
  333.4 19.7 %custom-call.50 = f32[2,128,128]{1,2,0:T(8,128)S(1)} custom-call(f32[2,128,128]{2,1,0:T(8,128)S(1)} %get-tuple-element.116), custom_call_target="InvertDiagBlocksLowerTriangular" | custom-call | tf_op jit(solution)/shard_map/jit(_solve_triangular)/triangular_solve | solution.py:24
  356.2 11.7 %cholesky.720 = f32[128,128]{1,0:T(8,128)S(1)} custom-call(f32[128,128]{1,0:T(8,128)S(1)} %cholesky.969), custom_call_target="Cholesky" | custom-call | tf_op jit(solution)/shard_map/jit(cholesky)/cholesky | solution.py:35
  368.5 9.8 %custom-call.52 = f32[1,128,128]{1,2,0:T(8,128)S(1)} custom-call(f32[1,128,128]{2,1,0:T(8,128)S(1)} %get-tuple-element.275), custom_call_target="InvertDiagBlocksLowerTriangular" | custom-call | tf_op jit(solution)/shard_map/jit(cholesky)/cholesky | solution.py:35
  378.9 12.1 %cholesky.737 = f32[128,128]{1,0:T(8,128)S(1)} custom-call(f32[128,128]{1,0:T(8,128)S(1)} %convolution_subtract_fusion.15), custom_call_target="Cholesky" | custom-call | tf_op jit(solution)/shard_map/jit(cholesky)/cholesky | solution.py:35
  393.6 4.1 while.39
  397.7 19.7 %custom-call.53 = f32[2,128,128]{1,2,0:T(8,128)S(1)} custom-call(f32[2,128,128]{2,1,0:T(8,128)S(1)} %get-tuple-element.118), custom_call_target="InvertDiagBlocksLowerTriangular" | custom-call | tf_op jit(solution)/shard_map/jit(_solve_triangular)/triangular_solve | solution.py:24
  421.9 9.8 %collective-permute-done.2 = f32[256,256]{1,0:T(8,128)S(1)} collective-permute-done((f32[256,256]{1,0:T(8,128)S(1)}, f32[256,256]{1,0:T(8,128)S(1)}, u32[]{:S(2)}, u32[]{:S(2)}) %collective-permute-start.2) | collective-permute-done | bytes 262176 | tf_op jit(solution)/shard_map/ppermute | solution.py:10
  432.5 11.7 %cholesky.754 = f32[128,128]{1,0:T(8,128)S(1)} custom-call(f32[128,128]{1,0:T(8,128)S(1)} %cholesky.972), custom_call_target="Cholesky" | custom-call | tf_op jit(solution)/shard_map/jit(cholesky)/cholesky | solution.py:32
  444.9 9.8 %custom-call.54 = f32[1,128,128]{1,2,0:T(8,128)S(1)} custom-call(f32[1,128,128]{2,1,0:T(8,128)S(1)} %get-tuple-element.271), custom_call_target="InvertDiagBlocksLowerTriangular" | custom-call | tf_op jit(solution)/shard_map/jit(cholesky)/cholesky | solution.py:32
  455.2 11.9 %cholesky.771 = f32[128,128]{1,0:T(8,128)S(1)} custom-call(f32[128,128]{1,0:T(8,128)S(1)} %slice_subtract_fusion.12), custom_call_target="Cholesky" | custom-call | tf_op jit(solution)/shard_map/jit(cholesky)/cholesky | solution.py:32
  469.0 3.8 while.40
  472.8 19.7 %custom-call.55 = f32[2,128,128]{1,2,0:T(8,128)S(1)} custom-call(f32[2,128,128]{2,1,0:T(8,128)S(1)} %get-tuple-element.119), custom_call_target="InvertDiagBlocksLowerTriangular" | custom-call | tf_op jit(solution)/shard_map/jit(_solve_triangular)/triangular_solve | solution.py:24
  495.6 11.7 %cholesky.788 = f32[128,128]{1,0:T(8,128)S(1)} custom-call(f32[128,128]{1,0:T(8,128)S(1)} %cholesky.975), custom_call_target="Cholesky" | custom-call | tf_op jit(solution)/shard_map/jit(cholesky)/cholesky | solution.py:35
  508.0 9.8 %custom-call.57 = f32[1,128,128]{1,2,0:T(8,128)S(1)} custom-call(f32[1,128,128]{2,1,0:T(8,128)S(1)} %get-tuple-element.267), custom_call_target="InvertDiagBlocksLowerTriangular" | custom-call | tf_op jit(solution)/shard_map/jit(cholesky)/cholesky | solution.py:35
  518.3 12.1 %cholesky.805 = f32[128,128]{1,0:T(8,128)S(1)} custom-call(f32[128,128]{1,0:T(8,128)S(1)} %convolution_subtract_fusion.14), custom_call_target="Cholesky" | custom-call | tf_op jit(solution)/shard_map/jit(cholesky)/cholesky | solution.py:35
  533.0 4.0 while.41
  536.9 19.7 %custom-call.58 = f32[2,128,128]{1,2,0:T(8,128)S(1)} custom-call(f32[2,128,128]{2,1,0:T(8,128)S(1)} %get-tuple-element.121), custom_call_target="InvertDiagBlocksLowerTriangular" | custom-call | tf_op jit(solution)/shard_map/jit(_solve_triangular)/triangular_solve | solution.py:24
  559.9 11.7 %cholesky.822 = f32[128,128]{1,0:T(8,128)S(1)} custom-call(f32[128,128]{1,0:T(8,128)S(1)} %cholesky.978), custom_call_target="Cholesky" | custom-call | tf_op jit(solution)/shard_map/jit(cholesky)/cholesky | solution.py:32
  572.3 9.8 %custom-call.59 = f32[1,128,128]{1,2,0:T(8,128)S(1)} custom-call(f32[1,128,128]{2,1,0:T(8,128)S(1)} %get-tuple-element.263), custom_call_target="InvertDiagBlocksLowerTriangular" | custom-call | tf_op jit(solution)/shard_map/jit(cholesky)/cholesky | solution.py:32
  582.6 11.9 %cholesky.839 = f32[128,128]{1,0:T(8,128)S(1)} custom-call(f32[128,128]{1,0:T(8,128)S(1)} %slice_subtract_fusion.11), custom_call_target="Cholesky" | custom-call | tf_op jit(solution)/shard_map/jit(cholesky)/cholesky | solution.py:32
  596.5 4.0 while.42
  600.5 19.7 %custom-call.60 = f32[2,128,128]{1,2,0:T(8,128)S(1)} custom-call(f32[2,128,128]{2,1,0:T(8,128)S(1)} %get-tuple-element.122), custom_call_target="InvertDiagBlocksLowerTriangular" | custom-call | tf_op jit(solution)/shard_map/jit(_solve_triangular)/triangular_solve | solution.py:24
  623.3 11.7 %cholesky.856 = f32[128,128]{1,0:T(8,128)S(1)} custom-call(f32[128,128]{1,0:T(8,128)S(1)} %cholesky.981), custom_call_target="Cholesky" | custom-call | tf_op jit(solution)/shard_map/jit(cholesky)/cholesky | solution.py:35
  635.7 9.8 %custom-call.62 = f32[1,128,128]{1,2,0:T(8,128)S(1)} custom-call(f32[1,128,128]{2,1,0:T(8,128)S(1)} %get-tuple-element.259), custom_call_target="InvertDiagBlocksLowerTriangular" | custom-call | tf_op jit(solution)/shard_map/jit(cholesky)/cholesky | solution.py:35
  646.0 12.1 %cholesky.873 = f32[128,128]{1,0:T(8,128)S(1)} custom-call(f32[128,128]{1,0:T(8,128)S(1)} %convolution_subtract_fusion.13), custom_call_target="Cholesky" | custom-call | tf_op jit(solution)/shard_map/jit(cholesky)/cholesky | solution.py:35
  664.3 19.7 %custom-call.63 = f32[2,128,128]{1,2,0:T(8,128)S(1)} custom-call(f32[2,128,128]{2,1,0:T(8,128)S(1)} %get-tuple-element.124), custom_call_target="InvertDiagBlocksLowerTriangular" | custom-call | tf_op jit(solution)/shard_map/jit(_solve_triangular)/triangular_solve | solution.py:24
  687.5 5.8 collective-permute-done.4
  694.1 11.7 %cholesky.890 = f32[128,128]{1,0:T(8,128)S(1)} custom-call(f32[128,128]{1,0:T(8,128)S(1)} %cholesky.984), custom_call_target="Cholesky" | custom-call | tf_op jit(solution)/shard_map/jit(cholesky)/cholesky | solution.py:32
  706.5 9.8 %custom-call.64 = f32[1,128,128]{1,2,0:T(8,128)S(1)} custom-call(f32[1,128,128]{2,1,0:T(8,128)S(1)} %get-tuple-element.255), custom_call_target="InvertDiagBlocksLowerTriangular" | custom-call | tf_op jit(solution)/shard_map/jit(cholesky)/cholesky | solution.py:32
  716.8 11.9 %cholesky.907 = f32[128,128]{1,0:T(8,128)S(1)} custom-call(f32[128,128]{1,0:T(8,128)S(1)} %slice_subtract_fusion.10), custom_call_target="Cholesky" | custom-call | tf_op jit(solution)/shard_map/jit(cholesky)/cholesky | solution.py:32
  730.7 3.9 while.44
  734.6 19.7 %custom-call.65 = f32[2,128,128]{1,2,0:T(8,128)S(1)} custom-call(f32[2,128,128]{2,1,0:T(8,128)S(1)} %get-tuple-element.125), custom_call_target="InvertDiagBlocksLowerTriangular" | custom-call | tf_op jit(solution)/shard_map/jit(_solve_triangular)/triangular_solve | solution.py:24
  757.4 11.7 %cholesky.924 = f32[128,128]{1,0:T(8,128)S(1)} custom-call(f32[128,128]{1,0:T(8,128)S(1)} %cholesky.987), custom_call_target="Cholesky" | custom-call | tf_op jit(solution)/shard_map/jit(cholesky)/cholesky | solution.py:35
  769.8 9.8 %custom-call.67 = f32[1,128,128]{1,2,0:T(8,128)S(1)} custom-call(f32[1,128,128]{2,1,0:T(8,128)S(1)} %get-tuple-element.251), custom_call_target="InvertDiagBlocksLowerTriangular" | custom-call | tf_op jit(solution)/shard_map/jit(cholesky)/cholesky | solution.py:35
  780.1 11.9 %cholesky.941 = f32[128,128]{1,0:T(8,128)S(1)} custom-call(f32[128,128]{1,0:T(8,128)S(1)} %convolution_subtract_fusion.12), custom_call_target="Cholesky" | custom-call | tf_op jit(solution)/shard_map/jit(cholesky)/cholesky | solution.py:35
  795.3 3.9 while.45
  799.2 19.7 %custom-call.68 = f32[2,128,128]{1,2,0:T(8,128)S(1)} custom-call(f32[2,128,128]{2,1,0:T(8,128)S(1)} %get-tuple-element.127), custom_call_target="InvertDiagBlocksLowerTriangular" | custom-call | tf_op jit(solution)/shard_map/jit(_solve_triangular)/triangular_solve | solution.py:24
  820.2 10.3 %convolution_multiply_fusion = f32[4096,256]{1,0:T(8,128)} fusion(f32[256,256]{1,0:T(8,128)S(1)} %fusion.60, f32[128,4096]{1,0:T(8,128)} %fusion.182, f32[128,4096]{1,0:T(8,128)S(1)} %copy-done.2), kind=kOutput, calls=%fused_computation.24 | convolution fusion | flops 3223322624 | bytes 8650752 | tf_op jit(solution)/shard_map/dot_general | solution.py:28
  (318 shorter events, 136.4 us)
Async XLA Ops:
  71.0 3.7 copy-start
  80.2 1.3 copy-start.3
  122.4 34.9 %collective-permute-start = (f32[256,256]{1,0:T(8,128)S(1)}, f32[256,256]{1,0:T(8,128)S(1)}, u32[]{:S(2)}, u32[]{:S(2)}) collective-permute-start(f32[256,256]{1,0:T(8,128)S(1)} %fusion.90), channel_id=1, source_target_pairs={{0,4},{4,0},{8,12},{12,8},{16,20},{20,16},{24,28},{28,24},{1,5},{5... | collective-permute-start | bytes 786440 | tf_op jit(solution)/shard_map/ppermute | solution.py:10
  149.4 2.0 copy-start.4
  151.4 1.9 copy-start.1
  284.0 7.8 collective-permute-start.1
  418.2 13.4 %collective-permute-start.2 = (f32[256,256]{1,0:T(8,128)S(1)}, f32[256,256]{1,0:T(8,128)S(1)}, u32[]{:S(2)}, u32[]{:S(2)}) collective-permute-start(f32[256,256]{1,0:T(8,128)S(1)} %fusion.94), channel_id=1, source_target_pairs={{0,16},{4,20},{8,24},{12,28},{16,0},{20,4},{24,8},{28,12},{1,17},{... | collective-permute-start | bytes 786440 | tf_op jit(solution)/shard_map/ppermute | solution.py:10
  557.5 1.6 collective-permute-start.3
  684.9 8.4 %collective-permute-start.4 = (f32[256,256]{1,0:T(8,128)S(1)}, f32[256,256]{1,0:T(8,128)S(1)}, u32[]{:S(2)}, u32[]{:S(2)}) collective-permute-start(f32[256,256]{1,0:T(8,128)S(1)} %fusion.96), channel_id=1, source_target_pairs={{0,2},{1,3},{2,0},{3,1},{4,6},{5,7},{6,4},{7,5},{8,10},{9,11},{10,... | collective-permute-start | bytes 786440 | tf_op jit(solution)/shard_map/ppermute | solution.py:10
  792.1 28.1 %copy-start.2 = (f32[128,4096]{1,0:T(8,128)S(1)}, f32[128,4096]{1,0:T(8,128)}, u32[]{:S(2)}) copy-start(f32[128,4096]{1,0:T(8,128)} %copy-done.1) | copy-start | bytes 6291460
where the time goes:
time: 835 us; the launch traced here: 831 us
  other arithmetic  655 us (78%)
  matrix products  76.1 us (9%)
  local copies, waits for them, and re-layouts  50.5 us (6%)
  waiting for transfers between devices  21.4 us (3%)
  between operations  17.7 us (2%)
  starting transfers between devices  8.93 us (1%)
    another operation x25, other arithmetic, whiten(): return jax.scipy.linalg.solve_triangular(lower, matrix.T, lower=True).T  237 us
    another operation x35, other arithmetic, merge_pair(): lower_two = jnp.linalg.cholesky(gram_of(own_one) + gram_of(other_one))  175 us
    another operation x35, other arithmetic, merge_pair(): lower_one = jnp.linalg.cholesky(gram_of(upper) + gram_of(partner))  174 us
    another operation x85, local copies, waits for them, and re-layouts, whiten(): return jax.scipy.linalg.solve_triangular(lower, matrix.T, lower=True).T  47.3 us
    another operation x7, other arithmetic, on_device(): lower_two = jnp.linalg.cholesky(gram_of(first))  34.8 us
    another operation x6, other arithmetic, on_device(): lower_one = jnp.linalg.cholesky(gram_of(panel))  34 us
    another operation x51, matrix products, whiten(): return jax.scipy.linalg.solve_triangular(lower, matrix.T, lower=True).T  30.8 us
    dot_general x22, matrix products, gram_of(): lax.dot_general(matrix, matrix, (((0,), (0,)), ((), ())), precision=lax.P...  23.7 us
  transfers between devices with their start and end apart: 5, of which 4 were waited for; matrix products, arithmetic and copies ran while one was open for 4% of the time, Pallas kernels for 0%

commit v1 on v0

v1 whole, which is shorter than its diff:
```python
import functools

import jax
import jax.numpy as jnp
from jax import lax
from jax.experimental import pallas as pl
from jax.experimental.pallas import tpu as pltpu
from jax.sharding import PartitionSpec as P

MESH = pl.DeviceIdType.MESH
F32 = jnp.float32
BF16 = jnp.bfloat16
VMEM_LIMIT = 48 * 1024 * 1024


def split3(value):
    high = value.astype(BF16)
    rest = value - high.astype(F32)
    mid = rest.astype(BF16)
    low = (rest - mid.astype(F32)).astype(BF16)
    return high, mid, low


def dot00(left, right):
    return lax.dot_general(left, right, (((0,), (0,)), ((), ())), preferred_element_type=F32)


def dot11(left, right):
    return lax.dot_general(left, right, (((1,), (1,)), ((), ())), preferred_element_type=F32)


def exact(left, right, dims):
    return lax.dot_general(
        left, right, (dims, ((), ())), precision=lax.Precision.HIGHEST, preferred_element_type=F32
    )


def gram_kernel(n_row, n_col, tile, a_ref, g_ref, buf, own, mixed, sum_ref, col_in, row_in, piece,
                load_sem, s1, r1, s2, r2, s3, r3, s4, r4):
    row, col = lax.axis_index("row"), lax.axis_index("col")
    rows, width = a_ref.shape
    tiles = rows // tile

    def load(step):
        return pltpu.make_async_copy(
            a_ref.at[pl.ds(step * tile, tile), :], buf.at[step], load_sem.at[step])

    for step in range(tiles):
        load(step).start()

    barrier = pltpu.get_barrier_semaphore()
    for d in range(1, n_col):
        pl.semaphore_signal(barrier, inc=1, device_id=(row, lax.rem(col + d, n_col)), device_id_type=MESH)
    for d in range(1, n_row):
        pl.semaphore_signal(barrier, inc=1, device_id=(lax.rem(row + d, n_row), col), device_id_type=MESH)

    own[...] = jnp.zeros_like(own)
    mixed[...] = jnp.zeros_like(mixed)
    for step in range(tiles):
        load(step).wait()
        high, mid, low = split3(buf[step])
        own[...] += dot00(high, high) + dot00(mid, mid)
        mixed[...] += dot00(high, mid) + dot00(high, low)
    own[...] += mixed[...] + mixed[...].T

    pl.semaphore_wait(barrier, n_col + n_row - 2)

    part = width // n_col
    copies = []
    for d in range(1, n_col):
        target = lax.rem(col + d, n_col)
        copy = pltpu.make_async_remote_copy(
            src_ref=own.at[pl.ds(pl.multiple_of(target * part, 8), part), :],
            dst_ref=col_in.at[d - 1],
            send_sem=s1.at[d - 1], recv_sem=r1.at[d - 1],
            device_id=(row, target), device_id_type=MESH)
        copy.start()
        copies.append(copy)
    total = own[pl.ds(pl.multiple_of(col * part, 8), part), :]
    for d in range(1, n_col):
        copies[d - 1].wait_recv()
        total += col_in[d - 1]
    sum_ref[...] = total
    pending = list(copies)

    if part % (8 * n_row) == 0:
        small = part // n_row
        copies = []
        for d in range(1, n_row):
            target = lax.rem(row + d, n_row)
            copy = pltpu.make_async_remote_copy(
                src_ref=sum_ref.at[pl.ds(pl.multiple_of(target * small, 8), small), :],
                dst_ref=row_in.at[d - 1],
                send_sem=s2.at[d - 1], recv_sem=r2.at[d - 1],
                device_id=(target, col), device_id_type=MESH)
            copy.start()
            copies.append(copy)
        total = sum_ref[pl.ds(pl.multiple_of(row * small, 8), small), :]
        for d in range(1, n_row):
            copies[d - 1].wait_recv()
            total += row_in[d - 1]
        piece[...] = total
        pending += copies
        mine = pl.ds(pl.multiple_of(col * part + row * small, 8), small)
        copies = []
        for d in range(1, n_row):
            copy = pltpu.make_async_remote_copy(
                src_ref=piece,
                dst_ref=g_ref.at[mine, :],
                send_sem=s3.at[d - 1], recv_sem=r3.at[d - 1],
                device_id=(lax.rem(row + d, n_row), col), device_id_type=MESH)
            copy.start()
            copies.append(copy)
        g_ref[mine, :] = total
        for copy in copies:
            copy.wait_recv()
        pending += copies
    else:
        copies = []
        for d in range(1, n_row):
            copy = pltpu.make_async_remote_copy(
                src_ref=sum_ref,
                dst_ref=row_in.at[row],
                send_sem=s2.at[d - 1], recv_sem=r2.at[d - 1],
                device_id=(lax.rem(row + d, n_row), col), device_id_type=MESH)
            copy.start()
            copies.append(copy)
        row_in[row] = total
        for copy in copies:
            copy.wait_recv()
        pending += copies
        total = row_in[0]
        for d in range(1, n_row):
            total += row_in[d]
        g_ref[pl.ds(pl.multiple_of(col * part, 8), part), :] = total

    mine = pl.ds(pl.multiple_of(col * part, 8), part)
    copies = []
    for d in range(1, n_col):
        copy = pltpu.make_async_remote_copy(
            src_ref=g_ref.at[mine, :],
            dst_ref=g_ref.at[mine, :],
            send_sem=s4.at[d - 1], recv_sem=r4.at[d - 1],
            device_id=(row, lax.rem(col + d, n_col)), device_id_type=MESH)
        copy.start()
        copies.append(copy)
    for copy in copies:
        copy.wait_recv()
    for copy in pending + copies:
        copy.wait_send()


def summed_gram(panel, collective_id):
    n_row, n_col = lax.axis_size("row"), lax.axis_size("col")
    rows, width = panel.shape
    tile = 512
    part = width // n_col
    scattered = part % (8 * n_row) == 0
    row_in = (n_row - 1, part // n_row, width) if scattered else (n_row, part, width)
    sems = []
    for count in (n_col, n_row, n_row, n_col):
        sems += [pltpu.SemaphoreType.DMA((count - 1,))] * 2
    return pl.pallas_call(
        functools.partial(gram_kernel, n_row, n_col, tile),
        out_shape=jax.ShapeDtypeStruct((width, width), F32),
        in_specs=[pl.BlockSpec(memory_space=pl.ANY)],
        out_specs=pl.BlockSpec(memory_space=pltpu.VMEM),
        scratch_shapes=[
            pltpu.VMEM((rows // tile, tile, width), F32),
            pltpu.VMEM((width, width), F32),
            pltpu.VMEM((width, width), F32),
            pltpu.VMEM((part, width), F32),
            pltpu.VMEM((n_col - 1, part, width), F32),
            pltpu.VMEM(row_in, F32),
            pltpu.VMEM((max(part // n_row, 8), width), F32),
            pltpu.SemaphoreType.DMA((rows // tile,)),
        ] + sems,
        compiler_params=pltpu.CompilerParams(
            collective_id=collective_id, has_side_effects=True, vmem_limit_bytes=VMEM_LIMIT),
        cost_estimate=pl.CostEstimate(
            flops=8 * rows * width * width, bytes_accessed=4 * rows * width, transcendentals=0),
        name="gram_sum",
    )(panel)


def eliminate(block, size):
    row_id = lax.broadcasted_iota(jnp.int32, (size, 2 * size), 0)
    col_id = lax.broadcasted_iota(jnp.int32, (size, 2 * size), 1)
    eye = (col_id == row_id + size).astype(F32)
    work = jnp.where(col_id < size, jnp.concatenate([block, block], axis=1), eye)
    scale = jnp.zeros((size, 1), F32)
    for k in range(size):
        column = work[:, k:k + 1]
        pivot_row = work[k:k + 1, :]
        pivot = work[k:k + 1, k:k + 1]
        inverse = 1.0 / pivot
        step = jnp.where(row_id[:, :1] > k, column * inverse, 0.0)
        work = work - step * pivot_row
        scale = jnp.where(row_id[:, :1] == k, pivot, scale)
    root = jnp.sqrt(scale)
    return work / root


def factor_into(g, work, upper):
    width = g.shape[0]
    size = min(64, width)
    work[...] = g[...]
    upper[...] = jnp.zeros_like(upper)
    tri_row = lax.broadcasted_iota(jnp.int32, (size, size), 0)
    tri_col = lax.broadcasted_iota(jnp.int32, (size, size), 1)
    for t in range(width // size):
        lo, hi = t * size, (t + 1) * size
        both = eliminate(work[lo:hi, lo:hi], size)
        diag = jnp.where(tri_col >= tri_row, both[:, :size], 0.0)
        inverse = jnp.where(tri_col <= tri_row, both[:, size:], 0.0)
        line = exact(inverse, work[lo:hi, :], ((1,), (0,)))
        upper[lo:hi, lo:hi] = diag
        if hi < width:
            upper[lo:hi, hi:] = line[:, hi:]
        work[lo:hi, :] = line
        work[lo:hi, lo:hi] = inverse
        if hi < width:
            work[lo:hi, lo:hi] = inverse
            work[hi:, lo:hi] = jnp.zeros((width - hi, size), F32)
            work[hi:, :] = work[hi:, :] - exact(line[:, hi:], work[lo:hi, :], ((0,), (0,)))
            work[lo:hi, hi:] = jnp.zeros((size, width - hi), F32)


def apply_kernel(total_rows, g_ref, a_ref, q_ref, factor_ref, work, upper, y_high, y_mid, y_low):
    @pl.when(pl.program_id(0) == 0)
    def _():
        factor_into(g_ref, work, upper)
        scale = jnp.sqrt(F32(total_rows))
        factor_ref[...] = upper[...] / scale
        high, mid, low = split3(work[...] * scale)
        y_high[...] = high
        y_mid[...] = mid
        y_low[...] = low

    high, mid, low = split3(a_ref[...])
    yh, ym, yl = y_high[...], y_mid[...], y_low[...]
    small = dot11(mid, ym) + dot11(high, yl) + dot11(low, yh)
    q_ref[...] = (small + dot11(high, ym) + dot11(mid, yh)) + dot11(high, yh)


def factor_and_apply(gram, panel, total_rows):
    rows, width = panel.shape
    tile = 512
    return pl.pallas_call(
        functools.partial(apply_kernel, total_rows),
        grid=(rows // tile,),
        out_shape=(
            jax.ShapeDtypeStruct((rows, width), F32),
            jax.ShapeDtypeStruct((width, width), F32),
        ),
        in_specs=[
            pl.BlockSpec((width, width), lambda i: (0, 0)),
            pl.BlockSpec((tile, width), lambda i: (i, 0)),
        ],
        out_specs=(
            pl.BlockSpec((tile, width), lambda i: (i, 0)),
            pl.BlockSpec((width, width), lambda i: (0, 0)),
        ),
        scratch_shapes=[
            pltpu.VMEM((width, width), F32),
            pltpu.VMEM((width, width), F32),
            pltpu.VMEM((width, width), BF16),
            pltpu.VMEM((width, width), BF16),
            pltpu.VMEM((width, width), BF16),
        ],
        compiler_params=pltpu.CompilerParams(vmem_limit_bytes=VMEM_LIMIT),
        cost_estimate=pl.CostEstimate(
            flops=12 * rows * width * width, bytes_accessed=8 * rows * width, transcendentals=0),
        name="factor_apply",
    )(gram, panel)


def on_device(panel):
    total_rows = panel.shape[0] * lax.axis_size("row") * lax.axis_size("col")
    gram = summed_gram(panel, 0)
    return factor_and_apply(gram, panel, total_rows)


def solution(mesh):
    return jax.shard_map(
        on_device,
        mesh=mesh,
        in_specs=(P(("row", "col"), None),),
        out_specs=(P(("row", "col"), None), P()),
        check_vma=False,
    )
```

time: 835 us -> 57.5 us (0.07)
  other arithmetic: 655 us -> 0 us
  matrix products: 76.1 us -> 0 us
  Pallas kernels: 0 us -> 54.5 us
  local copies, waits for them, and re-layouts: 50.5 us -> 2.18 us
  waiting for transfers between devices: 21.4 us -> 0 us
  between operations: 17.7 us -> 0.65 us
  starting transfers between devices: 8.93 us -> 0 us
    another operation x108 -> x0, other arithmetic: 655 us -> none  [the longest x25 237 us: whiten(): return jax.scipy.linalg.solve_triangular(lower, matrix.T, lower=True).T]
    pallas_call x0 -> x2, Pallas kernels: none -> 54.5 us  [the longest x1 32.1 us: factor_and_apply(): pl.pallas_call(functools.partial(apply_kernel, total_rows), grid=(rows //...]
    another operation x109 -> x0, local copies, waits for them, and re-layouts: 47.6 us -> none  [the longest x85 47.3 us: whiten(): return jax.scipy.linalg.solve_triangular(lower, matrix.T, lower=True).T]
    dot_general x34 -> x0, matrix products: 39.7 us -> none  [the longest x22 23.7 us: gram_of(): lax.dot_general(matrix, matrix, (((0,), (0,)), ((), ())), precision=lax.P...]
    another operation x75 -> x0, matrix products: 36.5 us -> none  [the longest x51 30.8 us: whiten(): return jax.scipy.linalg.solve_triangular(lower, matrix.T, lower=True).T]
    ppermute x5 -> x0, waiting for transfers between devices: 21.4 us -> none  [from_partner(): return lax.ppermute(value, axis, pairs)]
    ppermute x5 -> x0, starting transfers between devices: 8.93 us -> none  [from_partner(): return lax.ppermute(value, axis, pairs)]
  transfers between devices with their start and end apart: 5 -> 0, of which waited for: 4 -> 0; matrix products, arithmetic and copies ran while one was open for 4% -> 0% of each run, Pallas kernels for 0% -> 0%
where the time goes in v1:
time: 57.5 us; the launch traced here: 57.3 us
  Pallas kernels  54.5 us (95%)
  local copies, waits for them, and re-layouts  2.18 us (4%)
  between operations  0.65 us (1%)
    pallas_call x1, Pallas kernels, factor_and_apply(): pl.pallas_call(functools.partial(apply_kernel, total_rows), grid=(rows //...  32.1 us
    pallas_call x1, Pallas kernels, summed_gram(): pl.pallas_call(functools.partial(gram_kernel, n_row, n_col, tile), out_sh...  22.3 us
    unnamed x2, local copies, waits for them, and re-layouts  2.18 us

profile of v1, /device:TPU:0, one launch (start us, length us, event | category | flops | bytes accessed | tf_op | source)
XLA Modules:
  0.0 57.3 jit_solution(8692295982079504043)
XLA Ops:
  0.6 0.0 copy-start
  0.6 2.2 %copy-done = f32[4096,256]{1,0:T(8,128)S(1)} copy-done((f32[4096,256]{1,0:T(8,128)S(1)}, f32[4096,256]{1,0:T(8,128)}, u32[]{:S(2)}) %copy-start) | copy-done | bytes 4194328
  2.8 22.3 %gram_sum.1.g_ref = f32[256,256]{1,0:T(8,128)S(1)} custom-call(f32[4096,256]{1,0:T(8,128)S(1)} %copy-done), custom_call_target="tpu_custom_call" | custom-call | flops 2147483648 | bytes 4194304 | tf_op jit(solution)/shard_map/gram_sum/pallas_call | solution.py:163
  25.2 32.1 %factor_apply.1 = (f32[4096,256]{1,0:T(8,128)}, f32[256,256]{1,0:T(8,128)}) custom-call(f32[256,256]{1,0:T(8,128)S(1)} %gram_sum.1.g_ref, f32[4096,256]{1,0:T(8,128)S(1)} %copy-done), custom_call_target="tpu_custom_call" | custom-call | flops 3221225472 | bytes 8388608 | tf_op jit(solution)/shard_map/factor_apply/pallas_call | solution.py:249
Async XLA Ops:
  0.6 2.2 %copy-start = (f32[4096,256]{1,0:T(8,128)S(1)}, f32[4096,256]{1,0:T(8,128)}, u32[]{:S(2)}) copy-start(f32[4096,256]{1,0:T(8,128)} %a_ref.3) | copy-start | bytes 12582916

commit v2 on v1

--- a/solution.py
+++ b/solution.py
@@ -10,7 +10,7 @@
 MESH = pl.DeviceIdType.MESH
 F32 = jnp.float32
 BF16 = jnp.bfloat16
-VMEM_LIMIT = 48 * 1024 * 1024
+VMEM_LIMIT = 60 * 1024 * 1024
 
 
 def split3(value):
@@ -35,9 +35,21 @@
     )
 
 
-def gram_kernel(n_row, n_col, tile, a_ref, g_ref, buf, own, mixed, sum_ref, col_in, row_in, piece,
+def gram_kernel(near, far, n_col, tile, a_ref, g_ref, buf, own, mixed, sum_ref, col_in, row_in, piece,
                 load_sem, s1, r1, s2, r2, s3, r3, s4, r4):
     row, col = lax.axis_index("row"), lax.axis_index("col")
+    plane = near * n_col
+    slow, fast = row // near, lax.rem(row, near)
+    place = fast * n_col + col
+
+    def in_plane(d):
+        target = lax.rem(place + d, plane)
+        return target, (slow * near + target // n_col, lax.rem(target, n_col))
+
+    def across(d):
+        target = lax.rem(slow + d, far)
+        return target, (target * near + fast, col)
+
     rows, width = a_ref.shape
     tiles = rows // tile
 
@@ -49,10 +61,10 @@
         load(step).start()
 
     barrier = pltpu.get_barrier_semaphore()
-    for d in range(1, n_col):
-        pl.semaphore_signal(barrier, inc=1, device_id=(row, lax.rem(col + d, n_col)), device_id_type=MESH)
-    for d in range(1, n_row):
-        pl.semaphore_signal(barrier, inc=1, device_id=(lax.rem(row + d, n_row), col), device_id_type=MESH)
+    for d in range(1, plane):
+        pl.semaphore_signal(barrier, inc=1, device_id=in_plane(d)[1], device_id_type=MESH)
+    for d in range(1, far):
+        pl.semaphore_signal(barrier, inc=1, device_id=across(d)[1], device_id_type=MESH)
 
     own[...] = jnp.zeros_like(own)
     mixed[...] = jnp.zeros_like(mixed)
@@ -63,52 +75,52 @@
         mixed[...] += dot00(high, mid) + dot00(high, low)
     own[...] += mixed[...] + mixed[...].T
 
-    pl.semaphore_wait(barrier, n_col + n_row - 2)
-
-    part = width // n_col
+    pl.semaphore_wait(barrier, plane + far - 2)
+
+    part = width // plane
     copies = []
-    for d in range(1, n_col):
-        target = lax.rem(col + d, n_col)
+    for d in range(1, plane):
+        target, device = in_plane(d)
         copy = pltpu.make_async_remote_copy(
             src_ref=own.at[pl.ds(pl.multiple_of(target * part, 8), part), :],
             dst_ref=col_in.at[d - 1],
             send_sem=s1.at[d - 1], recv_sem=r1.at[d - 1],
-            device_id=(row, target), device_id_type=MESH)
+            device_id=device, device_id_type=MESH)
         copy.start()
         copies.append(copy)
-    total = own[pl.ds(pl.multiple_of(col * part, 8), part), :]
-    for d in range(1, n_col):
+    total = own[pl.ds(pl.multiple_of(place * part, 8), part), :]
+    for d in range(1, plane):
         copies[d - 1].wait_recv()
         total += col_in[d - 1]
     sum_ref[...] = total
     pending = list(copies)
 
-    if part % (8 * n_row) == 0:
-        small = part // n_row
+    if part % (8 * far) == 0:
+        small = part // far
         copies = []
-        for d in range(1, n_row):
-            target = lax.rem(row + d, n_row)
+        for d in range(1, far):
+            target, device = across(d)
             copy = pltpu.make_async_remote_copy(
                 src_ref=sum_ref.at[pl.ds(pl.multiple_of(target * small, 8), small), :],
                 dst_ref=row_in.at[d - 1],
                 send_sem=s2.at[d - 1], recv_sem=r2.at[d - 1],
-                device_id=(target, col), device_id_type=MESH)
+                device_id=device, device_id_type=MESH)
             copy.start()
             copies.append(copy)
-        total = sum_ref[pl.ds(pl.multiple_of(row * small, 8), small), :]
-        for d in range(1, n_row):
+        total = sum_ref[pl.ds(pl.multiple_of(slow * small, 8), small), :]
+        for d in range(1, far):
             copies[d - 1].wait_recv()
             total += row_in[d - 1]
         piece[...] = total
         pending += copies
-        mine = pl.ds(pl.multiple_of(col * part + row * small, 8), small)
+        mine = pl.ds(pl.multiple_of(place * part + slow * small, 8), small)
         copies = []
-        for d in range(1, n_row):
+        for d in range(1, far):
             copy = pltpu.make_async_remote_copy(
                 src_ref=piece,
                 dst_ref=g_ref.at[mine, :],
                 send_sem=s3.at[d - 1], recv_sem=r3.at[d - 1],
-                device_id=(lax.rem(row + d, n_row), col), device_id_type=MESH)
+                device_id=across(d)[1], device_id_type=MESH)
             copy.start()
             copies.append(copy)
         g_ref[mine, :] = total
@@ -117,31 +129,31 @@
         pending += copies
     else:
         copies = []
-        for d in range(1, n_row):
+        for d in range(1, far):
             copy = pltpu.make_async_remote_copy(
                 src_ref=sum_ref,
-                dst_ref=row_in.at[row],
+                dst_ref=row_in.at[slow],
                 send_sem=s2.at[d - 1], recv_sem=r2.at[d - 1],
-                device_id=(lax.rem(row + d, n_row), col), device_id_type=MESH)
+                device_id=across(d)[1], device_id_type=MESH)
             copy.start()
             copies.append(copy)
-        row_in[row] = total
+        row_in[slow] = total
         for copy in copies:
             copy.wait_recv()
         pending += copies
         total = row_in[0]
-        for d in range(1, n_row):
+        for d in range(1, far):
             total += row_in[d]
-        g_ref[pl.ds(pl.multiple_of(col * part, 8), part), :] = total
-
-    mine = pl.ds(pl.multiple_of(col * part, 8), part)
+        g_ref[pl.ds(pl.multiple_of(place * part, 8), part), :] = total
+
+    mine = pl.ds(pl.multiple_of(place * part, 8), part)
     copies = []
-    for d in range(1, n_col):
+    for d in range(1, plane):
         copy = pltpu.make_async_remote_copy(
             src_ref=g_ref.at[mine, :],
             dst_ref=g_ref.at[mine, :],
             send_sem=s4.at[d - 1], recv_sem=r4.at[d - 1],
-            device_id=(row, lax.rem(col + d, n_col)), device_id_type=MESH)
+            device_id=in_plane(d)[1], device_id_type=MESH)
         copy.start()
         copies.append(copy)
     for copy in copies:
@@ -154,14 +166,17 @@
     n_row, n_col = lax.axis_size("row"), lax.axis_size("col")
     rows, width = panel.shape
     tile = 512
-    part = width // n_col
-    scattered = part % (8 * n_row) == 0
-    row_in = (n_row - 1, part // n_row, width) if scattered else (n_row, part, width)
+    near = 2 ** ((n_row.bit_length() - 1) // 2)
+    far = n_row // near
+    plane = near * n_col
+    part = width // plane
+    scattered = part % (8 * far) == 0
+    row_in = (far - 1, part // far, width) if scattered else (far, part, width)
     sems = []
-    for count in (n_col, n_row, n_row, n_col):
+    for count in (plane, far, far, plane):
         sems += [pltpu.SemaphoreType.DMA((count - 1,))] * 2
     return pl.pallas_call(
-        functools.partial(gram_kernel, n_row, n_col, tile),
+        functools.partial(gram_kernel, near, far, n_col, tile),
         out_shape=jax.ShapeDtypeStruct((width, width), F32),
         in_specs=[pl.BlockSpec(memory_space=pl.ANY)],
         out_specs=pl.BlockSpec(memory_space=pltpu.VMEM),
@@ -170,9 +185,9 @@
             pltpu.VMEM((width, width), F32),
             pltpu.VMEM((width, width), F32),
             pltpu.VMEM((part, width), F32),
-            pltpu.VMEM((n_col - 1, part, width), F32),
+            pltpu.VMEM((plane - 1, part, width), F32),
             pltpu.VMEM(row_in, F32),
-            pltpu.VMEM((max(part // n_row, 8), width), F32),
+            pltpu.VMEM((max(part // far, 8), width), F32),
             pltpu.SemaphoreType.DMA((rows // tile,)),
         ] + sems,
         compiler_params=pltpu.CompilerParams(
@@ -183,22 +198,46 @@
     )(panel)
 
 
+def refined_reciprocal(value):
+    guess = pl.reciprocal(value, approx=True)
+    guess = guess * (2.0 - value * guess)
+    return guess * (2.0 - value * guess)
+
+
 def eliminate(block, size):
-    row_id = lax.broadcasted_iota(jnp.int32, (size, 2 * size), 0)
-    col_id = lax.broadcasted_iota(jnp.int32, (size, 2 * size), 1)
+    wide = 2 * size
+    row_id = lax.broadcasted_iota(jnp.int32, (size, wide), 0)
+    col_id = lax.broadcasted_iota(jnp.int32, (size, wide), 1)
     eye = (col_id == row_id + size).astype(F32)
     work = jnp.where(col_id < size, jnp.concatenate([block, block], axis=1), eye)
-    scale = jnp.zeros((size, 1), F32)
-    for k in range(size):
-        column = work[:, k:k + 1]
-        pivot_row = work[k:k + 1, :]
-        pivot = work[k:k + 1, k:k + 1]
-        inverse = 1.0 / pivot
-        step = jnp.where(row_id[:, :1] > k, column * inverse, 0.0)
-        work = work - step * pivot_row
-        scale = jnp.where(row_id[:, :1] == k, pivot, scale)
-    root = jnp.sqrt(scale)
-    return work / root
+    tile_row = lax.broadcasted_iota(jnp.int32, (8, wide), 0)
+    done = []
+    for first in range(0, size, 8):
+        left = size - first
+        columns = [
+            jnp.broadcast_to(work[:, first + j:first + j + 1], (left, wide)) for j in range(8)
+        ]
+        heads = [column[:8] for column in columns]
+        tails = [column[8:] for column in columns]
+        head, tail = work[:8], work[8:]
+        pivots = jnp.zeros((8, wide), F32)
+        for k in range(8):
+            pivot = jnp.broadcast_to(heads[k][k:k + 1], (8, wide))
+            inverse = refined_reciprocal(pivot)
+            pivots = jnp.where(tile_row == k, pivot, pivots)
+            line = head[k:k + 1] * inverse[:1]
+            step = jnp.where(tile_row > k, heads[k], 0.0)
+            head = head - step * line
+            if left > 8:
+                tail = tail - tails[k] * line
+            for j in range(k + 1, 8):
+                ratio = heads[j][k:k + 1] * inverse[:1]
+                if left > 8:
+                    tails[j] = tails[j] - tails[k] * ratio
+                heads[j] = heads[j] - step * ratio
+        done.append(head / jnp.sqrt(pivots))
+        work = tail
+    return jnp.concatenate(done, axis=0)
 
 
 def factor_into(g, work, upper):

time: 57.5 us -> 45.2 us (0.79)
  Pallas kernels: 54.5 us -> 44.3 us
  local copies, waits for them, and re-layouts: 2.18 us -> 0 us
    pallas_call x1, Pallas kernels: 32.1 us -> 21.2 us  [factor_and_apply(): pl.pallas_call(functools.partial(apply_kernel, total_rows), grid=(rows //...]
    unnamed x2 -> x0, local copies, waits for them, and re-layouts: 2.18 us -> none
    pallas_call x1, Pallas kernels: 22.3 us -> 23.1 us  [summed_gram(): pl.pallas_call(functools.partial(gram_kernel, near, far, n_col, tile), ou...]
where the time goes in v2:
time: 45.2 us; the launch traced here: 45 us
  Pallas kernels  44.3 us (98%)
  between operations  0.64 us (1%)
    pallas_call x1, Pallas kernels, summed_gram(): pl.pallas_call(functools.partial(gram_kernel, near, far, n_col, tile), ou...  23.1 us
    pallas_call x1, Pallas kernels, factor_and_apply(): pl.pallas_call(functools.partial(apply_kernel, total_rows), grid=(rows //...  21.2 us

profile of v2, /device:TPU:0, one launch (start us, length us, event | category | flops | bytes accessed | tf_op | source)
XLA Modules:
  0.0 45.0 jit_solution(4311440693358845110)
XLA Ops:
  0.6 23.1 %gram_sum.1.g_ref = f32[256,256]{1,0:T(8,128)} custom-call(f32[4096,256]{1,0:T(8,128)} %a_ref.3), custom_call_target="tpu_custom_call" | custom-call | flops 2147483648 | bytes 4194304 | tf_op jit(solution)/shard_map/gram_sum/pallas_call | solution.py:178
  23.8 21.2 %factor_apply.1 = (f32[4096,256]{1,0:T(8,128)}, f32[256,256]{1,0:T(8,128)}) custom-call(f32[256,256]{1,0:T(8,128)} %gram_sum.1.g_ref, f32[4096,256]{1,0:T(8,128)} %a_ref.3), custom_call_target="tpu_custom_call" | custom-call | flops 3221225472 | bytes 8388608 | tf_op jit(solution)/shard_map/factor_apply/pallas_call | solution.py:288

commit v3 on v2

--- a/solution.py
+++ b/solution.py
@@ -35,8 +35,8 @@
     )
 
 
-def gram_kernel(near, far, n_col, tile, a_ref, g_ref, buf, own, mixed, sum_ref, col_in, row_in, piece,
-                load_sem, s1, r1, s2, r2, s3, r3, s4, r4):
+def gram_kernel(near, far, n_col, tile, a_ref, g_ref, buf, own, mixed, sum_ref, col_in, row_in,
+                load_sem, s1, r1, s2, r2, s4, r4):
     row, col = lax.axis_index("row"), lax.axis_index("col")
     plane = near * n_col
     slow, fast = row // near, lax.rem(row, near)
@@ -73,11 +73,18 @@
         high, mid, low = split3(buf[step])
         own[...] += dot00(high, high) + dot00(mid, mid)
         mixed[...] += dot00(high, mid) + dot00(high, low)
-    own[...] += mixed[...] + mixed[...].T
+    whole = own[...] + (mixed[...] + mixed[...].T)
+    if g_ref.shape[0] < width:
+        half, quarter = width // 2, width // 4
+        own[:half, :] = whole[:half, :]
+        own[half:half + quarter, :half] = whole[half:half + quarter, half:]
+        own[half:half + quarter, half:] = whole[half + quarter:, half:]
+    else:
+        own[...] = whole
 
     pl.semaphore_wait(barrier, plane + far - 2)
 
-    part = width // plane
+    part = g_ref.shape[0] // plane
     copies = []
     for d in range(1, plane):
         target, device = in_plane(d)
@@ -95,56 +102,23 @@
     sum_ref[...] = total
     pending = list(copies)
 
-    if part % (8 * far) == 0:
-        small = part // far
-        copies = []
-        for d in range(1, far):
-            target, device = across(d)
-            copy = pltpu.make_async_remote_copy(
-                src_ref=sum_ref.at[pl.ds(pl.multiple_of(target * small, 8), small), :],
-                dst_ref=row_in.at[d - 1],
-                send_sem=s2.at[d - 1], recv_sem=r2.at[d - 1],
-                device_id=device, device_id_type=MESH)
-            copy.start()
-            copies.append(copy)
-        total = sum_ref[pl.ds(pl.multiple_of(slow * small, 8), small), :]
-        for d in range(1, far):
-            copies[d - 1].wait_recv()
-            total += row_in[d - 1]
-        piece[...] = total
-        pending += copies
-        mine = pl.ds(pl.multiple_of(place * part + slow * small, 8), small)
-        copies = []
-        for d in range(1, far):
-            copy = pltpu.make_async_remote_copy(
-                src_ref=piece,
-                dst_ref=g_ref.at[mine, :],
-                send_sem=s3.at[d - 1], recv_sem=r3.at[d - 1],
-                device_id=across(d)[1], device_id_type=MESH)
-            copy.start()
-            copies.append(copy)
-        g_ref[mine, :] = total
-        for copy in copies:
-            copy.wait_recv()
-        pending += copies
-    else:
-        copies = []
-        for d in range(1, far):
-            copy = pltpu.make_async_remote_copy(
-                src_ref=sum_ref,
-                dst_ref=row_in.at[slow],
-                send_sem=s2.at[d - 1], recv_sem=r2.at[d - 1],
-                device_id=across(d)[1], device_id_type=MESH)
-            copy.start()
-            copies.append(copy)
-        row_in[slow] = total
-        for copy in copies:
-            copy.wait_recv()
-        pending += copies
-        total = row_in[0]
-        for d in range(1, far):
-            total += row_in[d]
-        g_ref[pl.ds(pl.multiple_of(place * part, 8), part), :] = total
+    copies = []
+    for d in range(1, far):
+        copy = pltpu.make_async_remote_copy(
+            src_ref=sum_ref,
+            dst_ref=row_in.at[slow],
+            send_sem=s2.at[d - 1], recv_sem=r2.at[d - 1],
+            device_id=across(d)[1], device_id_type=MESH)
+        copy.start()
+        copies.append(copy)
+    row_in[slow] = total
+    for copy in copies:
+        copy.wait_recv()
+    pending += copies
+    total = row_in[0]
+    for d in range(1, far):
+        total += row_in[d]
+    g_ref[pl.ds(pl.multiple_of(place * part, 8), part), :] = total
 
     mine = pl.ds(pl.multiple_of(place * part, 8), part)
     copies = []
@@ -169,15 +143,16 @@
     near = 2 ** ((n_row.bit_length() - 1) // 2)
     far = n_row // near
     plane = near * n_col
-    part = width // plane
-    scattered = part % (8 * far) == 0
-    row_in = (far - 1, part // far, width) if scattered else (far, part, width)
+    packed = 3 * width // 4
+    if packed % (8 * plane) or width % 256:
+        packed = width
+    part = packed // plane
     sems = []
-    for count in (plane, far, far, plane):
+    for count in (plane, far, plane):
         sems += [pltpu.SemaphoreType.DMA((count - 1,))] * 2
     return pl.pallas_call(
         functools.partial(gram_kernel, near, far, n_col, tile),
-        out_shape=jax.ShapeDtypeStruct((width, width), F32),
+        out_shape=jax.ShapeDtypeStruct((packed, width), F32),
         in_specs=[pl.BlockSpec(memory_space=pl.ANY)],
         out_specs=pl.BlockSpec(memory_space=pltpu.VMEM),
         scratch_shapes=[
@@ -186,8 +161,7 @@
             pltpu.VMEM((width, width), F32),
             pltpu.VMEM((part, width), F32),
             pltpu.VMEM((plane - 1, part, width), F32),
-            pltpu.VMEM(row_in, F32),
-            pltpu.VMEM((max(part // far, 8), width), F32),
+            pltpu.VMEM((far, part, width), F32),
             pltpu.SemaphoreType.DMA((rows // tile,)),
         ] + sems,
         compiler_params=pltpu.CompilerParams(
@@ -241,9 +215,16 @@
 
 
 def factor_into(g, work, upper):
-    width = g.shape[0]
+    width = g.shape[1]
     size = min(64, width)
-    work[...] = g[...]
+    if g.shape[0] < width:
+        half, quarter = width // 2, width // 4
+        work[:half, :] = g[:half, :]
+        work[half:, :half] = jnp.zeros((half, half), F32)
+        work[half:half + quarter, half:] = g[half:, :half]
+        work[half + quarter:, half:] = g[half:, half:]
+    else:
+        work[...] = g[...]
     upper[...] = jnp.zeros_like(upper)
     tri_row = lax.broadcasted_iota(jnp.int32, (size, size), 0)
     tri_col = lax.broadcasted_iota(jnp.int32, (size, size), 1)
@@ -265,51 +246,61 @@
             work[lo:hi, hi:] = jnp.zeros((size, width - hi), F32)
 
 
-def apply_kernel(total_rows, g_ref, a_ref, q_ref, factor_ref, work, upper, y_high, y_mid, y_low):
-    @pl.when(pl.program_id(0) == 0)
-    def _():
-        factor_into(g_ref, work, upper)
-        scale = jnp.sqrt(F32(total_rows))
-        factor_ref[...] = upper[...] / scale
-        high, mid, low = split3(work[...] * scale)
-        y_high[...] = high
-        y_mid[...] = mid
-        y_low[...] = low
-
-    high, mid, low = split3(a_ref[...])
-    yh, ym, yl = y_high[...], y_mid[...], y_low[...]
-    small = dot11(mid, ym) + dot11(high, yl) + dot11(low, yh)
-    q_ref[...] = (small + dot11(high, ym) + dot11(mid, yh)) + dot11(high, yh)
+def apply_kernel(total_rows, tile, g_ref, a_ref, q_ref, factor_ref, work, upper, a_buf, q_buf, in_sem, out_sem):
+    tiles = a_ref.shape[0] // tile
+
+    def load(step):
+        return pltpu.make_async_copy(
+            a_ref.at[pl.ds(step * tile, tile), :], a_buf.at[step], in_sem.at[step])
+
+    def store(step):
+        return pltpu.make_async_copy(
+            q_buf.at[step], q_ref.at[pl.ds(step * tile, tile), :], out_sem.at[step])
+
+    for step in range(tiles):
+        load(step).start()
+    factor_into(g_ref, work, upper)
+    scale = jnp.sqrt(F32(total_rows))
+    factor_ref[...] = upper[...] / scale
+    y_high, y_mid, _ = split3(work[...] * scale)
+    for step in range(tiles):
+        load(step).wait()
+        high, mid, _ = split3(a_buf[step])
+        q_buf[step] = (dot11(high, y_mid) + dot11(mid, y_high)) + dot11(high, y_high)
+        store(step).start()
+    for step in range(tiles):
+        store(step).wait()
 
 
 def factor_and_apply(gram, panel, total_rows):
     rows, width = panel.shape
     tile = 512
+    tiles = rows // tile
     return pl.pallas_call(
-        functools.partial(apply_kernel, total_rows),
-        grid=(rows // tile,),
+        functools.partial(apply_kernel, total_rows, tile),
         out_shape=(
             jax.ShapeDtypeStruct((rows, width), F32),
             jax.ShapeDtypeStruct((width, width), F32),
         ),
         in_specs=[
-            pl.BlockSpec((width, width), lambda i: (0, 0)),
-            pl.BlockSpec((tile, width), lambda i: (i, 0)),
+            pl.BlockSpec(memory_space=pltpu.VMEM),
+            pl.BlockSpec(memory_space=pl.ANY),
         ],
         out_specs=(
-            pl.BlockSpec((tile, width), lambda i: (i, 0)),
-            pl.BlockSpec((width, width), lambda i: (0, 0)),
+            pl.BlockSpec(memory_space=pl.ANY),
+            pl.BlockSpec(memory_space=pltpu.VMEM),
         ),
         scratch_shapes=[
             pltpu.VMEM((width, width), F32),
             pltpu.VMEM((width, width), F32),
-            pltpu.VMEM((width, width), BF16),
-            pltpu.VMEM((width, width), BF16),
-            pltpu.VMEM((width, width), BF16),
+            pltpu.VMEM((tiles, tile, width), F32),
+            pltpu.VMEM((tiles, tile, width), F32),
+            pltpu.SemaphoreType.DMA((tiles,)),
+            pltpu.SemaphoreType.DMA((tiles,)),
         ],
         compiler_params=pltpu.CompilerParams(vmem_limit_bytes=VMEM_LIMIT),
         cost_estimate=pl.CostEstimate(
-            flops=12 * rows * width * width, bytes_accessed=8 * rows * width, transcendentals=0),
+            flops=6 * rows * width * width, bytes_accessed=8 * rows * width, transcendentals=0),
         name="factor_apply",
     )(gram, panel)
 

time: 45.2 us -> 40.6 us (0.90)
  Pallas kernels: 44.3 us -> 39.8 us
    pallas_call x1, Pallas kernels: 23.1 us -> 20.2 us  [summed_gram(): pl.pallas_call(functools.partial(gram_kernel, near, far, n_col, tile), ou...]
    pallas_call x1, Pallas kernels: 21.2 us -> 19.6 us  [factor_and_apply(): pl.pallas_call(functools.partial(apply_kernel, total_rows, tile), out_sha...]
where the time goes in v3:
time: 40.6 us; the launch traced here: 40.4 us
  Pallas kernels  39.8 us (98%)
  between operations  0.64 us (2%)
    pallas_call x1, Pallas kernels, summed_gram(): pl.pallas_call(functools.partial(gram_kernel, near, far, n_col, tile), ou...  20.2 us
    pallas_call x1, Pallas kernels, factor_and_apply(): pl.pallas_call(functools.partial(apply_kernel, total_rows, tile), out_sha...  19.6 us

profile of v3, /device:TPU:0, one launch (start us, length us, event | category | flops | bytes accessed | tf_op | source)
XLA Modules:
  0.0 40.4 jit_solution(10340667135950894889)
XLA Ops:
  0.6 20.2 %gram_sum.1.g_ref = f32[192,256]{1,0:T(8,128)} custom-call(f32[4096,256]{1,0:T(8,128)} %a_ref.3), custom_call_target="tpu_custom_call" | custom-call | flops 2147483648 | bytes 4194304 | tf_op jit(solution)/shard_map/gram_sum/pallas_call | solution.py:153
  20.8 19.6 %factor_apply.1 = (f32[4096,256]{1,0:T(8,128)}, f32[256,256]{1,0:T(8,128)}) custom-call(f32[192,256]{1,0:T(8,128)} %gram_sum.1.g_ref, f32[4096,256]{1,0:T(8,128)} %a_ref.3), custom_call_target="tpu_custom_call" | custom-call | flops 1610612736 | bytes 8388608 | tf_op jit(solution)/shard_map/factor_apply/pallas_call | solution.py:279

commit v4 on v3

--- a/solution.py
+++ b/solution.py
@@ -172,13 +172,7 @@
     )(panel)
 
 
-def refined_reciprocal(value):
-    guess = pl.reciprocal(value, approx=True)
-    guess = guess * (2.0 - value * guess)
-    return guess * (2.0 - value * guess)
-
-
-def eliminate(block, size):
+def eliminate(block, size, between):
     wide = 2 * size
     row_id = lax.broadcasted_iota(jnp.int32, (size, wide), 0)
     col_id = lax.broadcasted_iota(jnp.int32, (size, wide), 1)
@@ -192,29 +186,33 @@
             jnp.broadcast_to(work[:, first + j:first + j + 1], (left, wide)) for j in range(8)
         ]
         heads = [column[:8] for column in columns]
-        tails = [column[8:] for column in columns]
-        head, tail = work[:8], work[8:]
-        pivots = jnp.zeros((8, wide), F32)
+        tails = [[column[i:i + 8] for i in range(8, left, 8)] for column in columns]
+        head, tail = work[:8], [work[i:i + 8] for i in range(8, left, 8)]
+        pivots = jnp.ones((8, wide), F32)
         for k in range(8):
-            pivot = jnp.broadcast_to(heads[k][k:k + 1], (8, wide))
-            inverse = refined_reciprocal(pivot)
-            pivots = jnp.where(tile_row == k, pivot, pivots)
-            line = head[k:k + 1] * inverse[:1]
+            rows = [jnp.broadcast_to(heads[j][k:k + 1], (8, wide)) for j in range(k, 8)]
+            line = jnp.broadcast_to(head[k:k + 1], (8, wide))
+            inverse = pl.reciprocal(rows[0], approx=True)
+            pivots = jnp.where(tile_row == k, rows[0], pivots)
             step = jnp.where(tile_row > k, heads[k], 0.0)
-            head = head - step * line
-            if left > 8:
-                tail = tail - tails[k] * line
             for j in range(k + 1, 8):
-                ratio = heads[j][k:k + 1] * inverse[:1]
-                if left > 8:
-                    tails[j] = tails[j] - tails[k] * ratio
-                heads[j] = heads[j] - step * ratio
+                heads[j] = heads[j] - (step * rows[j - k]) * inverse
+            head = head - (step * line) * inverse
+            scaled_line = line * inverse
+            scaled_rows = [row * inverse for row in rows]
+            for i in range(len(tail)):
+                tail[i] = tail[i] - tails[k][i] * scaled_line
+                for j in range(k + 1, 8):
+                    tails[j][i] = tails[j][i] - tails[k][i] * scaled_rows[j - k]
         done.append(head / jnp.sqrt(pivots))
-        work = tail
+        if tail:
+            work = jnp.concatenate(tail, axis=0)
+        if between:
+            between[first // 8]()
     return jnp.concatenate(done, axis=0)
 
 
-def factor_into(g, work, upper):
+def factor_into(g, work, upper, before, between):
     width = g.shape[1]
     size = min(64, width)
     if g.shape[0] < width:
@@ -230,7 +228,9 @@
     tri_col = lax.broadcasted_iota(jnp.int32, (size, size), 1)
     for t in range(width // size):
         lo, hi = t * size, (t + 1) * size
-        both = eliminate(work[lo:hi, lo:hi], size)
+        if t in before:
+            before[t]()
+        both = eliminate(work[lo:hi, lo:hi], size, between.get(t))
         diag = jnp.where(tri_col >= tri_row, both[:, :size], 0.0)
         inverse = jnp.where(tri_col <= tri_row, both[:, size:], 0.0)
         line = exact(inverse, work[lo:hi, :], ((1,), (0,)))
@@ -246,36 +246,66 @@
             work[lo:hi, hi:] = jnp.zeros((size, width - hi), F32)
 
 
-def apply_kernel(total_rows, tile, g_ref, a_ref, q_ref, factor_ref, work, upper, a_buf, q_buf, in_sem, out_sem):
-    tiles = a_ref.shape[0] // tile
+def apply_kernel(total_rows, tile, g_ref, a_ref, q_ref, factor_ref, work, upper, a_buf, a_high, a_mid,
+                 y_wide, q_buf, in_sem, out_sem):
+    rows, width = a_ref.shape
+    tiles, half = rows // tile, width // 2
+    scale = jnp.sqrt(F32(total_rows))
 
     def load(step):
         return pltpu.make_async_copy(
             a_ref.at[pl.ds(step * tile, tile), :], a_buf.at[step], in_sem.at[step])
 
-    def store(step):
+    def store(step, side):
         return pltpu.make_async_copy(
-            q_buf.at[step], q_ref.at[pl.ds(step * tile, tile), :], out_sem.at[step])
+            q_buf.at[step, :, pl.ds(side * half, half)],
+            q_ref.at[pl.ds(step * tile, tile), pl.ds(side * half, half)],
+            out_sem.at[side, step])
+
+    def loaded():
+        for step in range(tiles):
+            load(step).wait()
+
+    def split(step):
+        a_high[step], a_mid[step], _ = split3(a_buf[step])
+
+    def prepare(side):
+        depth = (side + 1) * half
+        y = (work[side * half:depth, :depth] * scale).T
+        y_wide[:depth, :half], y_wide[:depth, half:], _ = split3(y)
+
+    def columns(side, step):
+        depth = (side + 1) * half
+        both = jnp.dot(a_high[step, :, :depth], y_wide[:depth, :], preferred_element_type=F32)
+        cross = jnp.dot(a_mid[step, :, :depth], y_wide[:depth, :half], preferred_element_type=F32)
+        q_buf[step, :, side * half:depth] = both[:, :half] + (both[:, half:] + cross)
+
+    def first_out():
+        for step in range(tiles):
+            store(step, 0).start()
 
     for step in range(tiles):
         load(step).start()
-    factor_into(g_ref, work, upper)
-    scale = jnp.sqrt(F32(total_rows))
+    before = {1: loaded, 2: functools.partial(prepare, 0), 3: first_out}
+    between = {
+        1: [functools.partial(split, step) for step in range(tiles)],
+        2: [functools.partial(columns, 0, step) for step in range(tiles)],
+    }
+    factor_into(g_ref, work, upper, before, between)
+    prepare(1)
+    for step in range(tiles):
+        columns(1, step)
+        store(step, 1).start()
     factor_ref[...] = upper[...] / scale
-    y_high, y_mid, _ = split3(work[...] * scale)
-    for step in range(tiles):
-        load(step).wait()
-        high, mid, _ = split3(a_buf[step])
-        q_buf[step] = (dot11(high, y_mid) + dot11(mid, y_high)) + dot11(high, y_high)
-        store(step).start()
-    for step in range(tiles):
-        store(step).wait()
+    for side in range(2):
+        for step in range(tiles):
+            store(step, side).wait()
 
 
 def factor_and_apply(gram, panel, total_rows):
     rows, width = panel.shape
-    tile = 512
-    tiles = rows // tile
+    tiles = 8
+    tile = rows // tiles
     return pl.pallas_call(
         functools.partial(apply_kernel, total_rows, tile),
         out_shape=(
@@ -294,9 +324,12 @@
             pltpu.VMEM((width, width), F32),
             pltpu.VMEM((width, width), F32),
             pltpu.VMEM((tiles, tile, width), F32),
+            pltpu.VMEM((tiles, tile, width), BF16),
+            pltpu.VMEM((tiles, tile, width), BF16),
+            pltpu.VMEM((width, width), BF16),
             pltpu.VMEM((tiles, tile, width), F32),
             pltpu.SemaphoreType.DMA((tiles,)),
-            pltpu.SemaphoreType.DMA((tiles,)),
+            pltpu.SemaphoreType.DMA((2, tiles)),
         ],
         compiler_params=pltpu.CompilerParams(vmem_limit_bytes=VMEM_LIMIT),
         cost_estimate=pl.CostEstimate(

time: 40.6 us -> 36.1 us (0.89)
  Pallas kernels: 39.8 us -> 35.3 us
    pallas_call x1, Pallas kernels: 19.6 us -> 15.1 us  [factor_and_apply(): pl.pallas_call(functools.partial(apply_kernel, total_rows, tile), out_sha...]
where the time goes in v4:
time: 36.1 us; the launch traced here: 35.9 us
  Pallas kernels  35.3 us (98%)
  between operations  0.64 us (2%)
    pallas_call x1, Pallas kernels, summed_gram(): pl.pallas_call(functools.partial(gram_kernel, near, far, n_col, tile), ou...  20.2 us
    pallas_call x1, Pallas kernels, factor_and_apply(): pl.pallas_call(functools.partial(apply_kernel, total_rows, tile), out_sha...  15.1 us

profile of v4, /device:TPU:0, one launch (start us, length us, event | category | flops | bytes accessed | tf_op | source)
XLA Modules:
  0.0 35.9 jit_solution(1480861617156722898)
XLA Ops:
  0.6 20.2 %gram_sum.1.g_ref = f32[192,256]{1,0:T(8,128)} custom-call(f32[4096,256]{1,0:T(8,128)} %a_ref.3), custom_call_target="tpu_custom_call" | custom-call | flops 2147483648 | bytes 4194304 | tf_op jit(solution)/shard_map/gram_sum/pallas_call | solution.py:153
  20.8 15.1 %factor_apply.1 = (f32[4096,256]{1,0:T(8,128)}, f32[256,256]{1,0:T(8,128)}) custom-call(f32[192,256]{1,0:T(8,128)} %gram_sum.1.g_ref, f32[4096,256]{1,0:T(8,128)} %a_ref.3), custom_call_target="tpu_custom_call" | custom-call | flops 1610612736 | bytes 8388608 | tf_op jit(solution)/shard_map/factor_apply/pallas_call | solution.py:309

commit v5 on v4

--- a/solution.py
+++ b/solution.py
@@ -85,55 +85,62 @@
     pl.semaphore_wait(barrier, plane + far - 2)
 
     part = g_ref.shape[0] // plane
-    copies = []
-    for d in range(1, plane):
+    half = width // 2
+    mine = pl.ds(pl.multiple_of(place * part, 8), part)
+    lanes = [pl.ds(0, half), pl.ds(half, half)]
+
+    def scatter(side, d):
         target, device = in_plane(d)
-        copy = pltpu.make_async_remote_copy(
-            src_ref=own.at[pl.ds(pl.multiple_of(target * part, 8), part), :],
-            dst_ref=col_in.at[d - 1],
-            send_sem=s1.at[d - 1], recv_sem=r1.at[d - 1],
+        return pltpu.make_async_remote_copy(
+            src_ref=own.at[pl.ds(pl.multiple_of(target * part, 8), part), lanes[side]],
+            dst_ref=col_in.at[side, d - 1],
+            send_sem=s1.at[side, d - 1], recv_sem=r1.at[side, d - 1],
             device_id=device, device_id_type=MESH)
-        copy.start()
-        copies.append(copy)
-    total = own[pl.ds(pl.multiple_of(place * part, 8), part), :]
-    for d in range(1, plane):
-        copies[d - 1].wait_recv()
-        total += col_in[d - 1]
-    sum_ref[...] = total
-    pending = list(copies)
-
-    copies = []
-    for d in range(1, far):
-        copy = pltpu.make_async_remote_copy(
-            src_ref=sum_ref,
-            dst_ref=row_in.at[slow],
-            send_sem=s2.at[d - 1], recv_sem=r2.at[d - 1],
+
+    def exchange(side, d):
+        return pltpu.make_async_remote_copy(
+            src_ref=sum_ref.at[side],
+            dst_ref=row_in.at[side, slow],
+            send_sem=s2.at[side, d - 1], recv_sem=r2.at[side, d - 1],
             device_id=across(d)[1], device_id_type=MESH)
-        copy.start()
-        copies.append(copy)
-    row_in[slow] = total
-    for copy in copies:
-        copy.wait_recv()
-    pending += copies
-    total = row_in[0]
-    for d in range(1, far):
-        total += row_in[d]
-    g_ref[pl.ds(pl.multiple_of(place * part, 8), part), :] = total
-
-    mine = pl.ds(pl.multiple_of(place * part, 8), part)
-    copies = []
-    for d in range(1, plane):
-        copy = pltpu.make_async_remote_copy(
-            src_ref=g_ref.at[mine, :],
-            dst_ref=g_ref.at[mine, :],
-            send_sem=s4.at[d - 1], recv_sem=r4.at[d - 1],
+
+    def gather(side, d):
+        return pltpu.make_async_remote_copy(
+            src_ref=g_ref.at[mine, lanes[side]],
+            dst_ref=g_ref.at[mine, lanes[side]],
+            send_sem=s4.at[side, d - 1], recv_sem=r4.at[side, d - 1],
             device_id=in_plane(d)[1], device_id_type=MESH)
-        copy.start()
-        copies.append(copy)
-    for copy in copies:
-        copy.wait_recv()
-    for copy in pending + copies:
-        copy.wait_send()
+
+    def start(make, side, count):
+        copies = [make(side, d) for d in range(1, count)]
+        for copy in copies:
+            copy.start()
+        return copies
+
+    scattered = [start(scatter, side, plane) for side in range(2)]
+    exchanged, gathered = [], []
+    for side in range(2):
+        total = own[mine, lanes[side]]
+        for d in range(1, plane):
+            scattered[side][d - 1].wait_recv()
+            total += col_in[side, d - 1]
+        sum_ref[side] = total
+        exchanged.append(start(exchange, side, far))
+        row_in[side, slow] = total
+    for side in range(2):
+        for copy in exchanged[side]:
+            copy.wait_recv()
+        total = row_in[side, 0]
+        for d in range(1, far):
+            total += row_in[side, d]
+        g_ref[mine, lanes[side]] = total
+        gathered.append(start(gather, side, plane))
+    for side in range(2):
+        for copy in gathered[side]:
+            copy.wait_recv()
+    for side in range(2):
+        for copy in scattered[side] + exchanged[side] + gathered[side]:
+            copy.wait_send()
 
 
 def summed_gram(panel, collective_id):
@@ -149,7 +156,7 @@
     part = packed // plane
     sems = []
     for count in (plane, far, plane):
-        sems += [pltpu.SemaphoreType.DMA((count - 1,))] * 2
+        sems += [pltpu.SemaphoreType.DMA((2, count - 1))] * 2
     return pl.pallas_call(
         functools.partial(gram_kernel, near, far, n_col, tile),
         out_shape=jax.ShapeDtypeStruct((packed, width), F32),
@@ -159,9 +166,9 @@
             pltpu.VMEM((rows // tile, tile, width), F32),
             pltpu.VMEM((width, width), F32),
             pltpu.VMEM((width, width), F32),
-            pltpu.VMEM((part, width), F32),
-            pltpu.VMEM((plane - 1, part, width), F32),
-            pltpu.VMEM((far, part, width), F32),
+            pltpu.VMEM((2, part, width // 2), F32),
+            pltpu.VMEM((2, plane - 1, part, width // 2), F32),
+            pltpu.VMEM((2, far, part, width // 2), F32),
             pltpu.SemaphoreType.DMA((rows // tile,)),
         ] + sems,
         compiler_params=pltpu.CompilerParams(

time: 36.1 us -> 36.1 us (level)
  no operation moved by 1% of the time
where the time goes in v5:
time: 36.1 us; the launch traced here: 35.9 us
  Pallas kernels  35.3 us (98%)
  between operations  0.64 us (2%)
    pallas_call x1, Pallas kernels, summed_gram(): pl.pallas_call(functools.partial(gram_kernel, near, far, n_col, tile), ou...  20.1 us
    pallas_call x1, Pallas kernels, factor_and_apply(): pl.pallas_call(functools.partial(apply_kernel, total_rows, tile), out_sha...  15.1 us

profile of v5, /device:TPU:0, one launch (start us, length us, event | category | flops | bytes accessed | tf_op | source)
XLA Modules:
  0.0 35.9 jit_solution(9243233029213497686)
XLA Ops:
  0.6 20.1 %gram_sum.1.g_ref = f32[192,256]{1,0:T(8,128)} custom-call(f32[4096,256]{1,0:T(8,128)} %a_ref.3), custom_call_target="tpu_custom_call" | custom-call | flops 2147483648 | bytes 4194304 | tf_op jit(solution)/shard_map/gram_sum/pallas_call | solution.py:160
  20.8 15.1 %factor_apply.1 = (f32[4096,256]{1,0:T(8,128)}, f32[256,256]{1,0:T(8,128)}) custom-call(f32[192,256]{1,0:T(8,128)} %gram_sum.1.g_ref, f32[4096,256]{1,0:T(8,128)} %a_ref.3), custom_call_target="tpu_custom_call" | custom-call | flops 1610612736 | bytes 8388608 | tf_op jit(solution)/shard_map/factor_apply/pallas_call | solution.py:316

commit v6 on v4

--- a/solution.py
+++ b/solution.py
@@ -139,7 +139,7 @@
 def summed_gram(panel, collective_id):
     n_row, n_col = lax.axis_size("row"), lax.axis_size("col")
     rows, width = panel.shape
-    tile = 512
+    tile = 1024
     near = 2 ** ((n_row.bit_length() - 1) // 2)
     far = n_row // near
     plane = near * n_col
@@ -247,7 +247,7 @@
 
 
 def apply_kernel(total_rows, tile, g_ref, a_ref, q_ref, factor_ref, work, upper, a_buf, a_high, a_mid,
-                 y_wide, q_buf, in_sem, out_sem):
+                 y_wide, q_buf, in_sem, out_sem, factor_sem):
     rows, width = a_ref.shape
     tiles, half = rows // tile, width // 2
     scale = jnp.sqrt(F32(total_rows))
@@ -293,10 +293,13 @@
     }
     factor_into(g_ref, work, upper, before, between)
     prepare(1)
+    upper[...] = upper[...] / scale
+    factor_out = pltpu.make_async_copy(upper, factor_ref, factor_sem)
+    factor_out.start()
     for step in range(tiles):
         columns(1, step)
         store(step, 1).start()
-    factor_ref[...] = upper[...] / scale
+    factor_out.wait()
     for side in range(2):
         for step in range(tiles):
             store(step, side).wait()
@@ -318,7 +321,7 @@
         ],
         out_specs=(
             pl.BlockSpec(memory_space=pl.ANY),
-            pl.BlockSpec(memory_space=pltpu.VMEM),
+            pl.BlockSpec(memory_space=pl.ANY),
         ),
         scratch_shapes=[
             pltpu.VMEM((width, width), F32),
@@ -330,6 +333,7 @@
             pltpu.VMEM((tiles, tile, width), F32),
             pltpu.SemaphoreType.DMA((tiles,)),
             pltpu.SemaphoreType.DMA((2, tiles)),
+            pltpu.SemaphoreType.DMA,
         ],
         compiler_params=pltpu.CompilerParams(vmem_limit_bytes=VMEM_LIMIT),
         cost_estimate=pl.CostEstimate(

time: 36.1 us -> 35.2 us (0.975)
  Pallas kernels: 35.3 us -> 34.4 us
    pallas_call x1, Pallas kernels: 15.1 us -> 14.5 us  [factor_and_apply(): pl.pallas_call(functools.partial(apply_kernel, total_rows, tile), out_sha...]
where the time goes in v6:
time: 35.2 us; the launch traced here: 35 us
  Pallas kernels  34.4 us (98%)
  between operations  0.64 us (2%)
    pallas_call x1, Pallas kernels, summed_gram(): pl.pallas_call(functools.partial(gram_kernel, near, far, n_col, tile), ou...  19.9 us
    pallas_call x1, Pallas kernels, factor_and_apply(): pl.pallas_call(functools.partial(apply_kernel, total_rows, tile), out_sha...  14.5 us

profile of v6, /device:TPU:0, one launch (start us, length us, event | category | flops | bytes accessed | tf_op | source)
XLA Modules:
  0.0 35.0 jit_solution(242254671118267521)
XLA Ops:
  0.6 19.9 %gram_sum.1.g_ref = f32[192,256]{1,0:T(8,128)} custom-call(f32[4096,256]{1,0:T(8,128)} %a_ref.3), custom_call_target="tpu_custom_call" | custom-call | flops 2147483648 | bytes 4194304 | tf_op jit(solution)/shard_map/gram_sum/pallas_call | solution.py:153
  20.5 14.5 %factor_apply.1 = (f32[4096,256]{1,0:T(8,128)}, f32[256,256]{1,0:T(8,128)}) custom-call(f32[192,256]{1,0:T(8,128)} %gram_sum.1.g_ref, f32[4096,256]{1,0:T(8,128)} %a_ref.3), custom_call_target="tpu_custom_call" | custom-call | flops 1610612736 | bytes 8388608 | tf_op jit(solution)/shard_map/factor_apply/pallas_call | solution.py:312
